TPU v7x, 128 devices: a whole 4x4x4 slice. The times are simulated.
128 devices in a mesh: tm: 4 (over x), mesh: 32 (over y, z, core).
Axes of the slice: x: 4, y: 4, z: 4, core: 2. Of those that a mesh axis runs over, the one named last changes fastest.
Arguments:
- right_sides: bfloat16 [8, 4096, 512], P('tm', 'mesh'), may hold values from -6 to 6
- diag_inverse: bfloat16 [8, 4096, 4096], P('tm', 'mesh'), may hold values from -0.09375 to 0.09375
- coupling: bfloat16 [8, 4096, 4096], P('tm', 'mesh'), may hold values from -0.0625 to 0.0625
- carry_in: bfloat16 [4096, 512], P('mesh'), may hold values from -6 to 6
- arrow_blocks: bfloat16 [8, 64, 4096], P('tm', None, 'mesh'), may hold values from -0.03125 to 0.03125
- tip_right: float32 [64, 512], replicated, may hold values from -6 to 6
- tip_inverse: float32 [64, 64], replicated, may hold values from -0.75 to 0.75
Outputs:
- forward_state: bfloat16 [8, 4096, 512], P('tm', 'mesh')
- tip_solution: float32 [64, 512], replicated
All inputs are finite; a program needn't handle non-finite values.
Results may differ from a plain program's by a relative error of at most 0.011.
Values may be sent and summed in bfloat16 or wider, within the bound.
A program may use at most 64 MiB of HBM per device.

v0:
```python
import jax
import jax.numpy as jnp
from jax import lax
from jax.sharding import PartitionSpec as P


def from_behind(block, axis, distance):
    devices = range(lax.axis_size(axis))
    route = [(i - distance, i) for i in devices if i - distance in devices]
    return lax.ppermute(block, axis, route)


def advance(matrix, source, earlier):
    coupled = jnp.dot(
        matrix,
        lax.all_gather(earlier, "mesh", axis=0, tiled=True),
        preferred_element_type=jnp.float32,
    )
    return (source - coupled).astype(jnp.bfloat16)


def body(right_sides, diag_inverse, coupling, carry_in, arrow_blocks, tip_right, tip_inverse):
    position = lax.axis_index("tm")
    devices_tm = lax.axis_size("tm")
    blocks, own_rows, columns = right_sides.shape
    scaled = jnp.einsum(
        "tij,tjr->tir",
        diag_inverse,
        lax.all_gather(right_sides, "mesh", axis=1, tiled=True),
        preferred_element_type=jnp.float32,
    )
    incoming = carry_in
    outputs = []
    for wave_step in range(devices_tm):
        current = incoming
        outputs = []
        for block_no in range(blocks):
            current = advance(coupling[block_no], scaled[block_no], current)
            outputs.append(current)
        if wave_step + 1 < devices_tm:
            moved = from_behind(current, "tm", 1)
            incoming = jnp.where(position == 0, carry_in, moved)
    solved = jnp.stack(outputs, axis=0)
    arrow_terms = jnp.einsum(
        "tfr,trs->fs", arrow_blocks, solved, preferred_element_type=jnp.float32
    )
    arrow_sum = lax.psum(arrow_terms, ("tm", "mesh"))
    tip_solution = jnp.dot(
        tip_inverse,
        tip_right - arrow_sum,
        precision=lax.Precision.HIGHEST,
        preferred_element_type=jnp.float32,
    )
    return (solved, tip_solution)


def solution(mesh):
    placed = (
        P("tm", "mesh", None),
        P("tm", "mesh", None),
        P("tm", "mesh", None),
        P("mesh", None),
        P("tm", None, "mesh"),
        P(),
        P(),
    )
    return jax.shard_map(
        body, mesh=mesh, in_specs=placed, out_specs=(P("tm", "mesh", None), P()), check_vma=False
    )
```

profile of v0, /device:TPU:1, one launch (start us, length us, event | category | flops | bytes accessed | tf_op | source)
XLA Modules:
  0.0 639.1 jit_solution(520782583988940051)
XLA Ops:
  7.2 0.0 all-gather.10.cloned.1.call-start
  7.2 0.7 all-gather.10.cloned.1.call-update
  7.9 0.0 all-gather.12.cloned.1.call-start
  8.0 0.7 all-gather.12.cloned.1.call-update
  8.7 0.0 all-gather.14.cloned.1.call-start
  8.7 58.4 %all-gather.10.cloned.1.call-done = bf16[2,4096,512]{2,1,0:T(8,128)(2,1)} async-done(((bf16[2,128,512]{2,1,0:T(8,128)(2,1)}), bf16[2,4096,512]{2,1,0:T(8,128)(2,1)}) %all-gather.10.cloned.1.call-update) | async-done | bytes 8388624 | tf_op jit(solution)/shard_map/all_gather | solution.py:29
  67.1 4.6 fusion.33
  71.8 43.6 %all-gather.12.cloned.1.call-done = bf16[4096,512]{1,0:T(8,128)(2,1)} async-done(((bf16[128,512]{1,0:T(8,128)(2,1)}), bf16[4096,512]{1,0:T(8,128)(2,1)}) %all-gather.12.cloned.1.call-update) | async-done | bytes 4194320 | tf_op jit(solution)/shard_map/all_gather | solution.py:16
  115.3 3.9 fusion.7
  119.2 0.0 all-gather.14.cloned.1.call-update
  119.2 0.0 all-gather.16.cloned.1.call-start
  119.3 45.8 %all-gather.14.cloned.1.call-done = bf16[4096,512]{1,0:T(8,128)(2,1)} async-done(((bf16[128,512]{1,0:T(8,128)(2,1)}), bf16[4096,512]{1,0:T(8,128)(2,1)}) %all-gather.14.cloned.1.call-update) | async-done | bytes 4194320 | tf_op jit(solution)/shard_map/all_gather | solution.py:16
  165.1 3.2 fusion.14
  168.3 3.1 collective-permute-start
  171.4 2.6 collective-permute-done
  174.0 0.7 broadcast_select_fusion.2
  174.7 0.0 all-gather.16.cloned.1.call-update
  174.7 0.0 all-gather.18.cloned.1.call-start
  174.8 47.6 %all-gather.16.cloned.1.call-done = bf16[4096,512]{1,0:T(8,128)(2,1)} async-done(((bf16[128,512]{1,0:T(8,128)(2,1)}), bf16[4096,512]{1,0:T(8,128)(2,1)}) %all-gather.16.cloned.1.call-update) | async-done | bytes 4194320 | tf_op jit(solution)/shard_map/all_gather | solution.py:16
  222.4 3.9 fusion.13
  226.3 0.0 all-gather.18.cloned.1.call-update
  226.3 0.0 all-gather.20.cloned.1.call-start
  226.4 45.8 %all-gather.18.cloned.1.call-done = bf16[4096,512]{1,0:T(8,128)(2,1)} async-done(((bf16[128,512]{1,0:T(8,128)(2,1)}), bf16[4096,512]{1,0:T(8,128)(2,1)}) %all-gather.18.cloned.1.call-update) | async-done | bytes 4194320 | tf_op jit(solution)/shard_map/all_gather | solution.py:16
  272.2 3.2 fusion.12
  275.4 3.1 collective-permute-start.1
  278.5 2.6 collective-permute-done.1
  281.1 0.7 broadcast_select_fusion.1
  281.8 0.0 all-gather.20.cloned.1.call-update
  281.8 0.0 all-gather.22.cloned.1.call-start
  281.9 47.6 %all-gather.20.cloned.1.call-done = bf16[4096,512]{1,0:T(8,128)(2,1)} async-done(((bf16[128,512]{1,0:T(8,128)(2,1)}), bf16[4096,512]{1,0:T(8,128)(2,1)}) %all-gather.20.cloned.1.call-update) | async-done | bytes 4194320 | tf_op jit(solution)/shard_map/all_gather | solution.py:16
  329.5 3.9 fusion.11
  333.4 0.0 all-gather.22.cloned.1.call-update
  333.4 0.0 all-gather.24.cloned.1.call-start
  333.4 45.8 %all-gather.22.cloned.1.call-done = bf16[4096,512]{1,0:T(8,128)(2,1)} async-done(((bf16[128,512]{1,0:T(8,128)(2,1)}), bf16[4096,512]{1,0:T(8,128)(2,1)}) %all-gather.22.cloned.1.call-update) | async-done | bytes 4194320 | tf_op jit(solution)/shard_map/all_gather | solution.py:16
  379.2 3.2 fusion.10
  382.5 3.1 collective-permute-start.2
  385.6 2.6 collective-permute-done.2
  388.2 0.7 broadcast_select_fusion
  388.9 0.0 all-gather.26.cloned.1.call-start
  389.0 47.6 %all-gather.24.cloned.1.call-done = bf16[4096,512]{1,0:T(8,128)(2,1)} async-done(((bf16[128,512]{1,0:T(8,128)(2,1)}), bf16[4096,512]{1,0:T(8,128)(2,1)}) %all-gather.24.cloned.1.call-update) | async-done | bytes 4194320 | tf_op jit(solution)/shard_map/all_gather | solution.py:16
  436.6 3.9 fusion.9
  440.5 0.0 all-gather.26.cloned.1.call-update
  440.5 0.0 all-reduce.2.cloned.1.call-start
  440.6 45.8 %all-gather.26.cloned.1.call-done = bf16[4096,512]{1,0:T(8,128)(2,1)} async-done(((bf16[128,512]{1,0:T(8,128)(2,1)}), bf16[4096,512]{1,0:T(8,128)(2,1)}) %all-gather.26.cloned.1.call-update) | async-done | bytes 4194320 | tf_op jit(solution)/shard_map/all_gather | solution.py:16
  486.4 3.2 fusion.15
  489.7 0.8 convolution_bitcast_fusion.7
  490.5 139.9 %all-reduce.2.cloned.1.call-done = f32[64,512]{1,0:T(8,128)} async-done(((f32[64,512]{1,0:T(8,128)}), f32[64,512]{1,0:T(8,128)}) %all-reduce.2.cloned.1.call-update) | async-done | bytes 131088 | tf_op jit(solution)/shard_map/psum | solution.py:47
  630.4 1.8 convolution_bitcast_fusion.8
  (17 shorter events, 0.1 us)
Async XLA Ops:
  7.2 60.0 %copy-start = (bf16[2,128,4096]{2,1,0:T(8,128)(2,1)S(1)}, bf16[2,128,4096]{2,1,0:T(8,128)(2,1)}, u32[]{:S(2)}) copy-start(bf16[2,128,4096]{2,1,0:T(8,128)(2,1)} %param.8) | copy-start | bytes 6291460
  7.2 59.9 %all-gather.10.cloned.1.call-start = ((), (), s32[]{:S(2)}) async-start(), calls=%async_computation | async-start | bytes 8650752 | tf_op jit(solution)/shard_map/all_gather | solution.py:29
  7.9 107.4 %all-gather.12.cloned.1.call-start = ((), (), s32[]{:S(2)}) async-start(), calls=%async_computation.1 | async-start | bytes 4325376 | tf_op jit(solution)/shard_map/all_gather | solution.py:16
  8.7 156.4 %all-gather.14.cloned.1.call-start = ((), (), s32[]{:S(2)}) async-start(), calls=%async_computation.2 | async-start | bytes 4325376 | tf_op jit(solution)/shard_map/all_gather | solution.py:16
  119.2 54.8 %copy-start.1 = (bf16[128,512]{1,0:T(8,128)(2,1)S(1)}, bf16[128,512]{1,0:T(8,128)(2,1)}, u32[]{:S(2)}) copy-start(bf16[128,512]{1,0:T(8,128)(2,1)} %param.10) | copy-start | bytes 393220
  119.2 103.2 %all-gather.16.cloned.1.call-start = ((), (), s32[]{:S(2)}) async-start(), calls=%async_computation.3 | async-start | bytes 4325376 | tf_op jit(solution)/shard_map/all_gather | solution.py:16
  168.3 5.7 collective-permute-start
  174.7 97.4 %all-gather.18.cloned.1.call-start = ((), (), s32[]{:S(2)}) async-start(), calls=%async_computation.4 | async-start | bytes 4325376 | tf_op jit(solution)/shard_map/all_gather | solution.py:16
  226.3 103.2 %all-gather.20.cloned.1.call-start = ((), (), s32[]{:S(2)}) async-start(), calls=%async_computation.5 | async-start | bytes 4325376 | tf_op jit(solution)/shard_map/all_gather | solution.py:16
  275.4 5.7 collective-permute-start.1
  281.8 97.4 %all-gather.22.cloned.1.call-start = ((), (), s32[]{:S(2)}) async-start(), calls=%async_computation.6 | async-start | bytes 4325376 | tf_op jit(solution)/shard_map/all_gather | solution.py:16
  333.4 103.2 %all-gather.24.cloned.1.call-start = ((), (), s32[]{:S(2)}) async-start(), calls=%async_computation.7 | async-start | bytes 4325376 | tf_op jit(solution)/shard_map/all_gather | solution.py:16
  382.5 5.7 collective-permute-start.2
  388.9 97.4 %all-gather.26.cloned.1.call-start = ((), (), s32[]{:S(2)}) async-start(), calls=%async_computation.8 | async-start | bytes 4325376 | tf_op jit(solution)/shard_map/all_gather | solution.py:16
  440.5 49.1 %copy-start.2 = (bf16[128,512]{1,0:T(8,128)(2,1)S(1)}, bf16[128,512]{1,0:T(8,128)(2,1)}, u32[]{:S(2)}) copy-start(bf16[128,512]{1,0:T(8,128)(2,1)} %fusion.9) | copy-start | bytes 393220
  440.5 49.2 %copy-start.5 = (bf16[2,64,128]{2,1,0:T(8,128)(2,1)S(1)}, bf16[2,64,128]{2,1,0:T(8,128)(2,1)}, u32[]{:S(2)}) copy-start(bf16[2,64,128]{2,1,0:T(8,128)(2,1)} %param.11) | copy-start | bytes 98308
  440.5 189.9 %copy-start.4 = (f32[64,512]{1,0:T(8,128)S(1)}, f32[64,512]{1,0:T(8,128)}, u32[]{:S(2)}) copy-start(f32[64,512]{1,0:T(8,128)} %param.12) | copy-start | bytes 393220
  440.5 189.9 %copy-start.6 = (f32[64,64]{1,0:T(8,128)S(1)}, f32[64,64]{1,0:T(8,128)}, u32[]{:S(2)}) copy-start(f32[64,64]{1,0:T(8,128)} %param.13) | copy-start | bytes 49156
  440.5 189.9 %all-reduce.2.cloned.1.call-start = ((), (), s32[]{:S(2)}) async-start(), calls=%async_computation.9 | async-start | bytes 262144 | tf_op jit(solution)/shard_map/psum | solution.py:47
  489.6 142.6 %copy-start.3 = (bf16[2,128,512]{2,1,0:T(8,128)(2,1)}, bf16[2,128,512]{2,1,0:T(8,128)(2,1)S(1)}, u32[]{:S(2)}) copy-start(bf16[2,128,512]{2,1,0:T(8,128)(2,1)S(1)} %pad_maximum_fusion) | copy-start | bytes 786436
Sparse Core Ops, SparseCore 0:
  10.4 56.6 all-gather.9
  69.4 45.8 all-gather.11
  119.4 45.6 all-gather.13
  174.8 47.5 all-gather.15
  226.4 45.6 all-gather.17
  281.9 47.4 all-gather.19
  333.5 45.6 all-gather.21
  389.0 47.5 all-gather.23
  440.6 45.6 all-gather.25
  491.5 138.8 all-reduce.1
where the time goes:
time: 639 us
  waiting for transfers between devices  577 us (90%)
  matrix products  35.8 us (6%)
  between operations  14.3 us (2%)
  starting transfers between devices  9.72 us (2%)
    all_gather x8, waiting for transfers between devices, advance(): lax.all_gather(earlier, 'mesh', axis=0, tiled=True)  370 us
    psum x1, waiting for transfers between devices, body(): arrow_sum = lax.psum(arrow_terms, ('tm', 'mesh'))  140 us
    all_gather x1, waiting for transfers between devices, body(): lax.all_gather(right_sides, 'mesh', axis=1, tiled=True)  58.4 us
    dot_general x8, matrix products, advance(): jnp.dot(matrix, lax.all_gather(earlier, 'mesh', axis=0, tiled=True), pref...  28.5 us
  transfers between devices with their start and end apart: 13, of which 13 were waited for; matrix products, arithmetic and copies ran while one was open for 1% of the time, Pallas kernels for 0%

commit v1 on v0

--- a/solution.py
+++ b/solution.py
@@ -44,7 +44,8 @@
     arrow_terms = jnp.einsum(
         "tfr,trs->fs", arrow_blocks, solved, preferred_element_type=jnp.float32
     )
-    arrow_sum = lax.psum(arrow_terms, ("tm", "mesh"))
+    shards = lax.all_gather(arrow_terms, ("tm", "mesh"))
+    arrow_sum = jnp.sum(shards, axis=0)
     tip_solution = jnp.dot(
         tip_inverse,
         tip_right - arrow_sum,

time: 639 us -> 586 us (0.917)
  waiting for transfers between devices: 577 us -> 517 us
  other arithmetic: 2.05 us -> 9.2 us
    psum x1 -> x0, waiting for transfers between devices: 140 us -> none  [body(): arrow_sum = lax.psum(arrow_terms, ('tm', 'mesh'))]
    all_gather x0 -> x1, waiting for transfers between devices: none -> 79.8 us  [body(): shards = lax.all_gather(arrow_terms, ('tm', 'mesh'))]
    reduce_sum x0 -> x1, other arithmetic: none -> 7.15 us  [body(): arrow_sum = jnp.sum(shards, axis=0)]
where the time goes in v1:
time: 586 us; the launch traced here: 585 us
  waiting for transfers between devices  517 us (88%)
  matrix products  34.9 us (6%)
  between operations  14.3 us (2%)
  starting transfers between devices  9.72 us (2%)
  other arithmetic  9.2 us (2%)
    all_gather x8, waiting for transfers between devices, advance(): lax.all_gather(earlier, 'mesh', axis=0, tiled=True)  370 us
    all_gather x1, waiting for transfers between devices, body(): shards = lax.all_gather(arrow_terms, ('tm', 'mesh'))  79.8 us
    all_gather x1, waiting for transfers between devices, body(): lax.all_gather(right_sides, 'mesh', axis=1, tiled=True)  58.4 us
    dot_general x8, matrix products, advance(): jnp.dot(matrix, lax.all_gather(earlier, 'mesh', axis=0, tiled=True), pref...  28.5 us
  transfers between devices with their start and end apart: 13, of which 13 were waited for; matrix products, arithmetic and copies ran while one was open for 1% of the time, Pallas kernels for 0%

profile of v1, /device:TPU:1, one launch (start us, length us, event | category | flops | bytes accessed | tf_op | source)
XLA Modules:
  0.0 585.2 jit_solution(5920308752114790513)
XLA Ops:
  7.2 0.0 all-gather.12.cloned.1.call-start
  7.2 0.7 all-gather.12.cloned.1.call-update
  7.9 0.0 all-gather.14.cloned.1.call-start
  8.0 0.7 all-gather.14.cloned.1.call-update
  8.7 0.0 all-gather.16.cloned.1.call-start
  8.7 58.4 %all-gather.12.cloned.1.call-done = bf16[2,4096,512]{2,1,0:T(8,128)(2,1)} async-done(((bf16[2,128,512]{2,1,0:T(8,128)(2,1)}), bf16[2,4096,512]{2,1,0:T(8,128)(2,1)}) %all-gather.12.cloned.1.call-update) | async-done | bytes 8388624 | tf_op jit(solution)/shard_map/all_gather | solution.py:29
  67.1 4.6 fusion.33
  71.8 43.6 %all-gather.14.cloned.1.call-done = bf16[4096,512]{1,0:T(8,128)(2,1)} async-done(((bf16[128,512]{1,0:T(8,128)(2,1)}), bf16[4096,512]{1,0:T(8,128)(2,1)}) %all-gather.14.cloned.1.call-update) | async-done | bytes 4194320 | tf_op jit(solution)/shard_map/all_gather | solution.py:16
  115.3 3.9 fusion.7
  119.2 0.0 all-gather.16.cloned.1.call-update
  119.2 0.0 all-gather.18.cloned.1.call-start
  119.3 45.8 %all-gather.16.cloned.1.call-done = bf16[4096,512]{1,0:T(8,128)(2,1)} async-done(((bf16[128,512]{1,0:T(8,128)(2,1)}), bf16[4096,512]{1,0:T(8,128)(2,1)}) %all-gather.16.cloned.1.call-update) | async-done | bytes 4194320 | tf_op jit(solution)/shard_map/all_gather | solution.py:16
  165.1 3.2 fusion.14
  168.3 3.1 collective-permute-start
  171.4 2.6 collective-permute-done
  174.0 0.7 broadcast_select_fusion.2
  174.7 0.0 all-gather.18.cloned.1.call-update
  174.7 0.0 all-gather.20.cloned.1.call-start
  174.8 47.6 %all-gather.18.cloned.1.call-done = bf16[4096,512]{1,0:T(8,128)(2,1)} async-done(((bf16[128,512]{1,0:T(8,128)(2,1)}), bf16[4096,512]{1,0:T(8,128)(2,1)}) %all-gather.18.cloned.1.call-update) | async-done | bytes 4194320 | tf_op jit(solution)/shard_map/all_gather | solution.py:16
  222.4 3.9 fusion.13
  226.3 0.0 all-gather.20.cloned.1.call-update
  226.3 0.0 all-gather.22.cloned.1.call-start
  226.4 45.8 %all-gather.20.cloned.1.call-done = bf16[4096,512]{1,0:T(8,128)(2,1)} async-done(((bf16[128,512]{1,0:T(8,128)(2,1)}), bf16[4096,512]{1,0:T(8,128)(2,1)}) %all-gather.20.cloned.1.call-update) | async-done | bytes 4194320 | tf_op jit(solution)/shard_map/all_gather | solution.py:16
  272.2 3.2 fusion.12
  275.4 3.1 collective-permute-start.1
  278.5 2.6 collective-permute-done.1
  281.1 0.7 broadcast_select_fusion.1
  281.8 0.0 all-gather.22.cloned.1.call-update
  281.8 0.0 all-gather.24.cloned.1.call-start
  281.9 47.6 %all-gather.22.cloned.1.call-done = bf16[4096,512]{1,0:T(8,128)(2,1)} async-done(((bf16[128,512]{1,0:T(8,128)(2,1)}), bf16[4096,512]{1,0:T(8,128)(2,1)}) %all-gather.22.cloned.1.call-update) | async-done | bytes 4194320 | tf_op jit(solution)/shard_map/all_gather | solution.py:16
  329.5 3.9 fusion.11
  333.4 0.0 all-gather.24.cloned.1.call-update
  333.4 0.0 all-gather.26.cloned.1.call-start
  333.4 45.8 %all-gather.24.cloned.1.call-done = bf16[4096,512]{1,0:T(8,128)(2,1)} async-done(((bf16[128,512]{1,0:T(8,128)(2,1)}), bf16[4096,512]{1,0:T(8,128)(2,1)}) %all-gather.24.cloned.1.call-update) | async-done | bytes 4194320 | tf_op jit(solution)/shard_map/all_gather | solution.py:16
  379.2 3.2 fusion.10
  382.5 3.1 collective-permute-start.2
  385.6 2.6 collective-permute-done.2
  388.2 0.7 broadcast_select_fusion
  388.9 0.0 all-gather.28.cloned.1.call-start
  389.0 47.6 %all-gather.26.cloned.1.call-done = bf16[4096,512]{1,0:T(8,128)(2,1)} async-done(((bf16[128,512]{1,0:T(8,128)(2,1)}), bf16[4096,512]{1,0:T(8,128)(2,1)}) %all-gather.26.cloned.1.call-update) | async-done | bytes 4194320 | tf_op jit(solution)/shard_map/all_gather | solution.py:16
  436.6 3.9 fusion.9
  440.5 0.0 all-gather.30.cloned.1.call-start
  440.5 45.8 %all-gather.28.cloned.1.call-done = bf16[4096,512]{1,0:T(8,128)(2,1)} async-done(((bf16[128,512]{1,0:T(8,128)(2,1)}), bf16[4096,512]{1,0:T(8,128)(2,1)}) %all-gather.28.cloned.1.call-update) | async-done | bytes 4194320 | tf_op jit(solution)/shard_map/all_gather | solution.py:16
  486.3 3.2 fusion.15
  489.6 0.8 convolution_bitcast_fusion.7
  490.5 79.8 %all-gather.30.cloned.1.call-done = f32[8192,512]{1,0:T(8,128)} async-done(((f32[64,512]{1,0:T(8,128)}), f32[8192,512]{1,0:T(8,128)}) %all-gather.30.cloned.1.call-update) | async-done | bytes 16777232 | tf_op jit(solution)/shard_map/all_gather | solution.py:47
  570.3 7.2 %reduce_sum.9 = f32[64,512]{1,0:T(8,128)S(1)} reduce(f32[128,64,512]{2,1,0:T(8,128)} %bitcast.105, f32[]{:T(128)} %constant.9.clone.1), dimensions={0}, to_apply=%region_0.1 | reduce | flops 4161536 | bytes 16908292 | tf_op jit(solution)/shard_map/reduce_sum | solution.py:48
  577.4 0.9 convolution_bitcast_fusion.8
  (18 shorter events, 0.1 us)
Async XLA Ops:
  7.2 60.0 %copy-start = (bf16[2,128,4096]{2,1,0:T(8,128)(2,1)S(1)}, bf16[2,128,4096]{2,1,0:T(8,128)(2,1)}, u32[]{:S(2)}) copy-start(bf16[2,128,4096]{2,1,0:T(8,128)(2,1)} %param.8) | copy-start | bytes 6291460
  7.2 59.9 %all-gather.12.cloned.1.call-start = ((), (), s32[]{:S(2)}) async-start(), calls=%async_computation | async-start | bytes 8650752 | tf_op jit(solution)/shard_map/all_gather | solution.py:29
  7.9 107.4 %all-gather.14.cloned.1.call-start = ((), (), s32[]{:S(2)}) async-start(), calls=%async_computation.1 | async-start | bytes 4325376 | tf_op jit(solution)/shard_map/all_gather | solution.py:16
  8.7 156.4 %all-gather.16.cloned.1.call-start = ((), (), s32[]{:S(2)}) async-start(), calls=%async_computation.2 | async-start | bytes 4325376 | tf_op jit(solution)/shard_map/all_gather | solution.py:16
  119.2 54.8 %copy-start.1 = (bf16[128,512]{1,0:T(8,128)(2,1)S(1)}, bf16[128,512]{1,0:T(8,128)(2,1)}, u32[]{:S(2)}) copy-start(bf16[128,512]{1,0:T(8,128)(2,1)} %param.10) | copy-start | bytes 393220
  119.2 103.2 %all-gather.18.cloned.1.call-start = ((), (), s32[]{:S(2)}) async-start(), calls=%async_computation.3 | async-start | bytes 4325376 | tf_op jit(solution)/shard_map/all_gather | solution.py:16
  168.3 5.7 collective-permute-start
  174.7 97.4 %all-gather.20.cloned.1.call-start = ((), (), s32[]{:S(2)}) async-start(), calls=%async_computation.4 | async-start | bytes 4325376 | tf_op jit(solution)/shard_map/all_gather | solution.py:16
  226.3 103.2 %all-gather.22.cloned.1.call-start = ((), (), s32[]{:S(2)}) async-start(), calls=%async_computation.5 | async-start | bytes 4325376 | tf_op jit(solution)/shard_map/all_gather | solution.py:16
  275.4 5.7 collective-permute-start.1
  281.8 97.4 %all-gather.24.cloned.1.call-start = ((), (), s32[]{:S(2)}) async-start(), calls=%async_computation.6 | async-start | bytes 4325376 | tf_op jit(solution)/shard_map/all_gather | solution.py:16
  333.4 103.2 %all-gather.26.cloned.1.call-start = ((), (), s32[]{:S(2)}) async-start(), calls=%async_computation.7 | async-start | bytes 4325376 | tf_op jit(solution)/shard_map/all_gather | solution.py:16
  382.5 5.7 collective-permute-start.2
  388.9 97.4 %all-gather.28.cloned.1.call-start = ((), (), s32[]{:S(2)}) async-start(), calls=%async_computation.8 | async-start | bytes 4325376 | tf_op jit(solution)/shard_map/all_gather | solution.py:16
  440.5 49.1 %copy-start.2 = (bf16[128,512]{1,0:T(8,128)(2,1)S(1)}, bf16[128,512]{1,0:T(8,128)(2,1)}, u32[]{:S(2)}) copy-start(bf16[128,512]{1,0:T(8,128)(2,1)} %fusion.9) | copy-start | bytes 393220
  440.5 49.2 %copy-start.5 = (bf16[2,64,128]{2,1,0:T(8,128)(2,1)S(1)}, bf16[2,64,128]{2,1,0:T(8,128)(2,1)}, u32[]{:S(2)}) copy-start(bf16[2,64,128]{2,1,0:T(8,128)(2,1)} %param.11) | copy-start | bytes 98308
  440.5 129.8 %all-gather.30.cloned.1.call-start = ((), (), s32[]{:S(2)}) async-start(), calls=%async_computation.9 | async-start | bytes 16908288 | tf_op jit(solution)/shard_map/all_gather | solution.py:47
  489.6 87.8 %copy-start.3 = (bf16[2,128,512]{2,1,0:T(8,128)(2,1)}, bf16[2,128,512]{2,1,0:T(8,128)(2,1)S(1)}, u32[]{:S(2)}) copy-start(bf16[2,128,512]{2,1,0:T(8,128)(2,1)S(1)} %pad_maximum_fusion) | copy-start | bytes 786436
  570.3 7.2 %copy-start.4 = (f32[64,512]{1,0:T(8,128)S(1)}, f32[64,512]{1,0:T(8,128)}, u32[]{:S(2)}) copy-start(f32[64,512]{1,0:T(8,128)} %param.12) | copy-start | bytes 393220
  570.3 7.2 %copy-start.6 = (f32[64,64]{1,0:T(8,128)S(1)}, f32[64,64]{1,0:T(8,128)}, u32[]{:S(2)}) copy-start(f32[64,64]{1,0:T(8,128)} %param.13) | copy-start | bytes 49156
Sparse Core Ops, SparseCore 0:
  10.4 56.6 all-gather.11
  69.4 45.8 all-gather.13
  119.4 45.6 all-gather.15
  174.8 47.5 all-gather.17
  226.4 45.6 all-gather.19
  281.9 47.4 all-gather.21
  333.5 45.6 all-gather.23
  389.0 47.5 all-gather.25
  440.6 45.6 all-gather.27
  490.6 79.5 all-gather.29
